TPU v7x, 512 devices: a whole 4x8x8 slice. The times are simulated.
512 devices in a mesh: region: 16 (over z, core), row: 32 (over x, y).
Axes of the slice: x: 4, y: 8, z: 8, core: 2. Of those that a mesh axis runs over, the one named last changes fastest.
Arguments:
- queries: float32 [64, 512], P('row'), may hold values from -6 to 6
- descriptors: float32 [131072, 512], P(('region', 'row')), may hold values from -6 to 6
- candidates: int32 [64, 64], replicated, may hold values from 0 to 1023
- cluster_perm: int32 [16, 8192], P('region', 'row'), may hold values from 0 to 8191, each once within a row
- tile_vals: float32 [6144, 128, 128], P(('region', 'row')), may hold values from 0 to 1, as said below
- tile_row: int32 [6144], P(('region', 'row')), may hold values from 0 to 1, as said below
- tile_col: int32 [6144], P(('region', 'row')), may hold values from 0 to 67, as said below
Outputs:
- diffused: float32 [64, 131072], P(None, ('region', 'row'))
- residual: float32 [64, 131072], P(None, ('region', 'row'))
Inputs may be any that keep to these rules, and one draw needn't show every extreme that they name: Each row of cluster_perm names every storage position of its region once. tile_row is a row tile of the owning device. In device (region r, row index i) the first 2 tiles are its diagonal tiles in order; the intra-region column tiles lie on row indices i, i + 1, i - 1, i + 3, i - 3, i + 8, i - 8 and i + 32 // 2 (modulo 32). `tile_col`: every device holds tiles with column slots in both neighbouring regions. `tile_vals`: S is symmetric with nonnegative entries and every row of S sums to at most 1.
All inputs are finite; a program needn't handle non-finite values.
Results may differ from a plain program's by a relative error of at most 0.0003.
Values sent between devices are 32-bit elements; how exact they have to be, the bound alone decides.
No kernel may reach another device: no remote copies, remote signals or barrier semaphores. Data moves between devices by JAX's collectives and lax.ppermute only.
A program may use at most 64 MiB of HBM per device.

v0:
```python
import jax
import jax.numpy as jnp
from jax import lax
from jax.sharding import PartitionSpec as P

ITERS = 3


def with_halo(block, sides, width):
    for axis, dim in sides:
        count = lax.axis_size(axis)
        forward = [(i, i + 1) for i in range(count - 1)]
        forward.append((count - 1, 0))
        backward = [(target, source) for source, target in forward]
        low = lax.ppermute(
            lax.slice_in_dim(block, block.shape[dim] - width, None, axis=dim), axis, forward
        )
        high = lax.ppermute(lax.slice_in_dim(block, 0, width, axis=dim), axis, backward)
        block = jnp.concatenate([low, block, high], axis=dim)
    return block


def apply_operator(direction, tile_vals, tile_row, tile_col):
    tile_size = tile_vals.shape[1]
    query_count = direction.shape[0]
    row_count = direction.shape[1]
    per_device = row_count // tile_size
    faces = with_halo(direction[None], (("region", 0),), 1)
    lower_face = faces[0]
    upper_face = faces[2]
    region_field = lax.all_gather(direction, "row", axis=1, tiled=True)
    joined = jnp.concatenate([region_field, lower_face, upper_face], axis=1)
    slots = joined.reshape(query_count, -1, tile_size).transpose(1, 0, 2)
    picked = slots[tile_col]
    products = jnp.einsum("tqc,trc->tqr", picked, tile_vals, precision=lax.Precision.HIGHEST)
    selector = (tile_row[None, :] == jnp.arange(per_device, dtype=jnp.int32)[:, None]).astype(
        jnp.float32
    )
    summed = jnp.einsum("at,tqr->qar", selector, products, precision=lax.Precision.HIGHEST).reshape(
        query_count, row_count
    )
    return direction - 0.9 * summed


def square_sum(residual):
    return lax.psum(jnp.sum(residual * residual, axis=1), ("region", "row"))


def local(queries, descriptors, candidates, cluster_perm, tile_vals, tile_row, tile_col):
    tile_size = tile_vals.shape[1]
    row_count = descriptors.shape[0]
    feature_width = descriptors.shape[1]
    per_device = row_count // tile_size
    n_row = lax.axis_size("row")
    device_id = lax.axis_index("region") * n_row + lax.axis_index("row")
    all_queries = lax.all_gather(queries, "row", axis=0, tiled=True)
    scores = lax.dot_general(
        all_queries,
        descriptors,
        (((1,), (1,)), ((), ())),
        precision=lax.Precision.HIGHEST,
        preferred_element_type=jnp.float32,
    ) * (1.0 / jnp.sqrt(jnp.float32(feature_width)))
    own_blocks = device_id * per_device + jnp.arange(per_device, dtype=jnp.int32)
    member = jnp.any(candidates[:, :, None] == own_blocks[None, None, :], axis=1)
    member_rows = jnp.repeat(member, tile_size, axis=1)
    stored = jnp.where(member_rows, jnp.exp(scores), jnp.float32(0.0))
    region_scores = lax.all_gather(stored, "row", axis=1, tiled=True)
    seeds = jnp.take(region_scores, cluster_perm[0], axis=1)
    diffused = jnp.zeros_like(seeds)
    residual = seeds
    direction = seeds
    norm_now = square_sum(residual)
    for step in range(ITERS):
        image = apply_operator(direction, tile_vals, tile_row, tile_col)
        curve = lax.psum(jnp.sum(direction * image, axis=1), ("region", "row"))
        alpha = norm_now / curve
        diffused = diffused + alpha[:, None] * direction
        residual = residual - alpha[:, None] * image
        if step + 1 < ITERS:
            norm_next = square_sum(residual)
            direction = residual + (norm_next / norm_now)[:, None] * direction
            norm_now = norm_next
    return (diffused, residual)


def solution(mesh):
    in_specs = (
        P("row", None),
        P(("region", "row"), None),
        P(),
        P("region", "row"),
        P(("region", "row"), None, None),
        P(("region", "row")),
        P(("region", "row")),
    )
    out_specs = (P(None, ("region", "row")), P(None, ("region", "row")))
    return jax.shard_map(local, mesh=mesh, in_specs=in_specs, out_specs=out_specs, check_vma=False)
```

profile of v0, /device:TPU:1, one launch (start us, length us, event | category | flops | bytes accessed | tf_op | source)
XLA Modules:
  0.0 883.6 jit_solution(5404740575829851799)
XLA Ops:
  7.2 1.0 compare_reduce_fusion
  8.2 0.1 copy.82
  8.4 32.4 %all-gather = f32[32,2,512]{2,1,0:T(2,128)S(1)} all-gather(f32[1,2,512]{2,1,0:T(2,128)} %bitcast.164), channel_id=1, replica_groups=mesh['region'=16,'row'=32] {'row'}, dimensions={0}, use_global_device_ids=true | all-gather | bytes 135168 | tf_op jit(solution)/shard_map/all_gather | solution.py:56
  40.8 0.1 broadcast_in_dim.27
  41.0 2.3 fusion.1
  43.3 0.7 compare_select_fusion
  44.0 0.7 compare_and_fusion.1
  44.7 85.5 %all-gather.6.cloned.1.call-done = f32[64,8192]{1,0:T(8,128)} async-done(((f32[64,256]{1,0:T(8,128)}), f32[64,8192]{1,0:T(8,128)}) %all-gather.6.cloned.1.call-update) | async-done | bytes 2097168 | tf_op jit(solution)/shard_map/all_gather | solution.py:68
  130.2 3.8 copy.83
  134.0 2.9 gather_fusion
  137.0 0.7 multiply_reduce_fusion.4
  137.9 4.8 collective-permute-start
  142.7 1.3 collective-permute-done
  144.0 2.4 collective-permute-done.1
  146.4 71.2 %all-gather.8.cloned.1.call-done = f32[64,8192]{1,0:T(8,128)} async-done(((f32[64,256]{1,0:T(8,128)}), f32[64,8192]{1,0:T(8,128)}) %all-gather.8.cloned.1.call-update) | async-done | bytes 2097168 | tf_op jit(solution)/shard_map/all_gather | solution.py:31
  217.6 1.9 bitcast_bitcast_fusion.2
  219.5 1.3 gather_fusion.1
  220.9 2.6 fusion.29
  223.5 0.6 fusion.6
  224.2 101.1 %all-reduce = (f32[64]{0:T(128)S(1)}, f32[64]{0:T(128)S(1)}) all-reduce(f32[64]{0:T(128)S(1)} %get-tuple-element.16, f32[64]{0:T(128)S(1)} %multiply_reduce_fusion.3), channel_id=1, replica_groups=mesh['region'=16,'row'=32] {'region','row'}, use_global_device_ids=true, to_apply=%region_2.3 | all-reduce | flops 128 | bytes 1024 | tf_op jit(solution)/shard_map/psum | solution.py:46
  325.3 0.2 multiply_reduce_fusion.2
  325.5 94.4 %psum.44 = f32[64]{0:T(128)S(1)} all-reduce(f32[64]{0:T(128)S(1)} %multiply_reduce_fusion.2), channel_id=1, replica_groups=mesh['region'=16,'row'=32] {'region','row'}, use_global_device_ids=true, to_apply=%region_6.7 | all-reduce | flops 64 | bytes 512 | tf_op jit(solution)/shard_map/psum | solution.py:46
  419.9 0.7 multiply_add_fusion.4
  421.0 1.2 collective-permute-start.2
  422.1 1.3 collective-permute-done.2
  423.5 2.7 collective-permute-done.3
  426.1 66.5 %all-gather.10.cloned.1.call-done = f32[64,8192]{1,0:T(8,128)} async-done(((f32[64,256]{1,0:T(8,128)}), f32[64,8192]{1,0:T(8,128)}) %all-gather.10.cloned.1.call-update) | async-done | bytes 2097168 | tf_op jit(solution)/shard_map/all_gather | solution.py:31
  492.6 1.9 bitcast_bitcast_fusion.1
  494.5 1.3 gather_fusion.2
  495.9 2.6 fusion.30
  498.5 0.6 fusion.4
  499.1 0.2 multiply_reduce_fusion.1
  499.3 101.1 %psum.45 = f32[64]{0:T(128)S(1)} all-reduce(f32[64]{0:T(128)S(1)} %multiply_reduce_fusion.1), channel_id=1, replica_groups=mesh['region'=16,'row'=32] {'region','row'}, use_global_device_ids=true, to_apply=%region_8.9 | all-reduce | flops 64 | bytes 512 | tf_op jit(solution)/shard_map/psum | solution.py:76
  600.4 0.2 multiply_reduce_fusion
  600.6 94.4 %psum.46 = f32[64]{0:T(128)S(1)} all-reduce(f32[64]{0:T(128)S(1)} %multiply_reduce_fusion), channel_id=1, replica_groups=mesh['region'=16,'row'=32] {'region','row'}, use_global_device_ids=true, to_apply=%region_10.11 | all-reduce | flops 64 | bytes 512 | tf_op jit(solution)/shard_map/psum | solution.py:46
  695.0 0.6 copy-done.13
  695.6 0.7 multiply_add_fusion.2
  696.6 1.2 collective-permute-start.4
  697.7 1.3 collective-permute-done.4
  699.1 2.7 collective-permute-done.5
  701.7 66.6 %all-gather.12.cloned.1.call-done = f32[64,8192]{1,0:T(8,128)} async-done(((f32[64,256]{1,0:T(8,128)}), f32[64,8192]{1,0:T(8,128)}) %all-gather.12.cloned.1.call-update) | async-done | bytes 2097168 | tf_op jit(solution)/shard_map/all_gather | solution.py:31
  768.3 1.9 bitcast_bitcast_fusion
  770.2 1.6 gather_fusion.3
  771.8 2.6 fusion.31
  774.4 0.6 fusion.2
  775.0 0.2 fusion.8
  775.2 101.1 %psum.47 = f32[64]{0:T(128)S(1)} all-reduce(f32[64]{0:T(128)S(1)} %fusion.8), channel_id=1, replica_groups=mesh['region'=16,'row'=32] {'region','row'}, use_global_device_ids=true, to_apply=%region_12.13 | all-reduce | flops 64 | bytes 512 | tf_op jit(solution)/shard_map/psum | solution.py:76
  876.4 0.8 fusion.10
  (62 shorter events, 1.1 us)
Async XLA Ops:
  7.2 213.7 %copy-start = (f32[12,128,128]{2,1,0:T(8,128)S(1)}, f32[12,128,128]{2,1,0:T(8,128)}, u32[]{:S(2)}) copy-start(f32[12,128,128]{2,1,0:T(8,128)} %param.11) | copy-start | bytes 2359300
  7.2 123.1 %all-gather.6.cloned.1.call-start = ((), (), s32[]{:S(2)}) async-start(), calls=%async_computation | async-start | bytes 2162688 | tf_op jit(solution)/shard_map/all_gather | solution.py:68
  43.3 174.3 %all-gather.8.cloned.1.call-start = ((), (), s32[]{:S(2)}) async-start(), calls=%async_computation.1 | async-start | bytes 2162688 | tf_op jit(solution)/shard_map/all_gather | solution.py:31
  44.7 376.1 %copy-start.4 = (pred[256]{0:T(512)(128)(4,1)}, pred[256]{0:T(512)(128)(4,1)S(1)}, u32[]{:S(2)}) copy-start(pred[256]{0:T(512)(128)(4,1)S(1)} %compare_and_fusion.1) | copy-start | bytes 772
  44.7 93.1 %copy-start.12 = (s32[12]{0:T(128)S(1)}, s32[12]{0:T(128)}, u32[]{:S(2)}) copy-start(s32[12]{0:T(128)} %param.13) | copy-start | bytes 148
  44.7 93.1 %copy-start.11 = (s32[1,256]{1,0:T(1,128)S(1)}, s32[1,256]{1,0:T(1,128)}, u32[]{:S(2)}) copy-start(s32[1,256]{1,0:T(1,128)} %param.10) | copy-start | bytes 3076
  137.8 354.8 %all-gather.10.cloned.1.call-start = ((), (), s32[]{:S(2)}) async-start(), calls=%async_computation.2 | async-start | bytes 2162688 | tf_op jit(solution)/shard_map/all_gather | solution.py:31
  137.9 6.1 collective-permute-start
  142.7 3.7 collective-permute-start.1
  142.7 351.8 %copy-start.6 = (s32[1024]{0:T(1024)}, s32[1024]{0:T(1024)S(1)}, u32[]{:S(2)}) copy-start(s32[1024]{0:T(1024)S(1)} %pad_clamp_fusion) | copy-start | bytes 12292
  219.5 4.0 copy-start.9
  219.5 200.4 %copy-start.1 = (f32[64,256]{1,0:T(8,128)S(1)}, f32[64,256]{1,0:T(8,128)}, u32[]{:S(2)}) copy-start(f32[64,256]{1,0:T(8,128)} %get-tuple-element.17) | copy-start | bytes 196612
  420.7 347.6 %all-gather.12.cloned.1.call-start = ((), (), s32[]{:S(2)}) async-start(), calls=%async_computation.3 | async-start | bytes 2162688 | tf_op jit(solution)/shard_map/all_gather | solution.py:31
  421.0 2.5 collective-permute-start.2
  422.1 4.0 collective-permute-start.3
  494.5 201.1 %copy-start.2 = (f32[64,256]{1,0:T(8,128)S(1)}, f32[64,256]{1,0:T(8,128)}, u32[]{:S(2)}) copy-start(f32[64,256]{1,0:T(8,128)} %multiply_add_fusion.4) | copy-start | bytes 196612
  495.9 200.6 %copy-start.5 = (pred[256]{0:T(512)(128)(4,1)S(1)}, pred[256]{0:T(512)(128)(4,1)}, u32[]{:S(2)}) copy-start(pred[256]{0:T(512)(128)(4,1)} %copy-done.4) | copy-start | bytes 772
  695.0 0.6 copy-start.13
  695.6 72.7 %copy-start.7 = (f32[64]{0:T(128)}, f32[64]{0:T(128)S(1)}, u32[]{:S(2)}) copy-start(f32[64]{0:T(128)S(1)} %div.18) | copy-start | bytes 772
  696.6 2.5 collective-permute-start.4
  697.7 4.0 collective-permute-start.5
  770.2 4.3 copy-start.10
  770.2 4.9 copy-start.8
  770.2 106.2 %copy-start.14 = (f32[64]{0:T(128)S(1)}, f32[64]{0:T(128)}, u32[]{:S(2)}) copy-start(f32[64]{0:T(128)} %copy-done.13) | copy-start | bytes 772
  770.2 106.2 %copy-start.3 = (f32[64,256]{1,0:T(8,128)S(1)}, f32[64,256]{1,0:T(8,128)}, u32[]{:S(2)}) copy-start(f32[64,256]{1,0:T(8,128)} %get-tuple-element.14) | copy-start | bytes 196612
Sparse Core Ops, SparseCore 0:
  43.4 86.7 all-gather.5
  137.9 79.6 all-gather.7
  420.8 71.7 all-gather.9
  696.4 71.7 all-gather.11
where the time goes:
time: 884 us
  blocking collectives  524 us (59%)
  waiting for transfers between devices  302 us (34%)
  between operations  14.1 us (2%)
  local copies, waits for them, and re-layouts  12.2 us (1%)
  other arithmetic  12.1 us (1%)
  matrix products  12 us (1%)
    psum x3, blocking collectives, square_sum(): return lax.psum(jnp.sum(residual * residual, axis=1), ('region', 'row'))  290 us
    all_gather x3, waiting for transfers between devices, apply_operator(): region_field = lax.all_gather(direction, 'row', axis=1, tiled=True)  204 us
    psum x2, blocking collectives, local(): curve = lax.psum(jnp.sum(direction * image, axis=1), ('region', 'row'))  202 us
    all_gather x1, waiting for transfers between devices, local(): region_scores = lax.all_gather(stored, 'row', axis=1, tiled=True)  85.5 us
    all_gather x1, blocking collectives, local(): all_queries = lax.all_gather(queries, 'row', axis=0, tiled=True)  32.4 us
  transfers between devices with their start and end apart: 10, of which 10 were waited for; matrix products, arithmetic and copies ran while one was open for 0% of the time, Pallas kernels for 0%

commit v1 on v0

--- a/solution.py
+++ b/solution.py
@@ -43,7 +43,7 @@
 
 
 def square_sum(residual):
-    return lax.psum(jnp.sum(residual * residual, axis=1), ("region", "row"))
+    return jnp.sum(lax.all_gather(jnp.sum(residual * residual, axis=1), ("region", "row")), axis=0)
 
 
 def local(queries, descriptors, candidates, cluster_perm, tile_vals, tile_row, tile_col):

time: 884 us -> 1470 us (1.66)
  waiting for transfers between devices: 302 us -> 1070 us
  blocking collectives: 524 us -> 336 us
    unnamed x4 -> x10, waiting for transfers between devices: 0.08 us -> 773 us
    psum x3 -> x0, blocking collectives: 290 us -> none  [square_sum(): return lax.psum(jnp.sum(residual * residual, axis=1), ('region', 'row'))]
    psum x2 -> x3, blocking collectives: 202 us -> 303 us  [local(): curve = lax.psum(jnp.sum(direction * image, axis=1), ('region', 'row'))]
  transfers between devices with their start and end apart: 10 -> 13, of which waited for: 10 -> 11; matrix products, arithmetic and copies ran while one was open for 0% -> 0% of each run, Pallas kernels for 0% -> 0%
where the time goes in v1:
time: 1470 us
  waiting for transfers between devices  1070 us (73%)
  blocking collectives  336 us (23%)
  local copies, waits for them, and re-layouts  17.9 us (1%)
    unnamed x10, waiting for transfers between devices  773 us
    psum x3, blocking collectives, local(): curve = lax.psum(jnp.sum(direction * image, axis=1), ('region', 'row'))  303 us
    all_gather x3, waiting for transfers between devices, apply_operator(): region_field = lax.all_gather(direction, 'row', axis=1, tiled=True)  207 us
    all_gather x1, waiting for transfers between devices, local(): region_scores = lax.all_gather(stored, 'row', axis=1, tiled=True)  85.5 us
    all_gather x1, blocking collectives, local(): all_queries = lax.all_gather(queries, 'row', axis=0, tiled=True)  32.4 us
  transfers between devices with their start and end apart: 13, of which 11 were waited for; matrix products, arithmetic and copies ran while one was open for 0% of the time, Pallas kernels for 0%

profile of v1, /device:TPU:1, one launch (start us, length us, event | category | flops | bytes accessed | tf_op | source)
XLA Modules:
  0.0 1473.2 jit_solution(9160891001898649088)
XLA Ops:
  7.2 1.0 compare_reduce_fusion
  8.4 32.4 %all-gather.3 = f32[32,2,512]{2,1,0:T(2,128)S(1)} all-gather(f32[1,2,512]{2,1,0:T(2,128)} %bitcast.164), channel_id=1, replica_groups=mesh['region'=16,'row'=32] {'row'}, dimensions={0}, use_global_device_ids=true | all-gather | bytes 135168 | tf_op jit(solution)/shard_map/all_gather | solution.py:56
  41.0 2.3 fusion.1
  43.4 0.7 compare_select_fusion
  44.0 0.7 compare_and_fusion.1
  44.7 85.5 %all-gather.9.cloned.1.call-done = f32[64,8192]{1,0:T(8,128)} async-done(((f32[64,256]{1,0:T(8,128)}), f32[64,8192]{1,0:T(8,128)}) %all-gather.9.cloned.1.call-update) | async-done | bytes 2097168 | tf_op jit(solution)/shard_map/all_gather | solution.py:68
  130.2 3.8 copy.83
  134.0 2.9 gather_fusion
  137.0 0.7 multiply_reduce_fusion.4
  138.0 0.6 copy-done.5
  138.8 0.7 all-gather.11.cloned.1.call-update
  139.6 4.8 collective-permute-start
  144.4 258.8 %all-reduce.7.cloned.1.call-done = f32[32768]{0:T(1024)} async-done(((f32[32768]{0:T(1024)}), f32[32768]{0:T(1024)}) %all-reduce.7.cloned.1.call-update) | async-done | bytes 131088
  403.2 1.0 reshape.422
  404.3 73.6 %all-gather.11.cloned.1.call-done = f32[64,8192]{1,0:T(8,128)} async-done(((f32[64,256]{1,0:T(8,128)}), f32[64,8192]{1,0:T(8,128)}) %all-gather.11.cloned.1.call-update) | async-done | bytes 2097168 | tf_op jit(solution)/shard_map/all_gather | solution.py:31
  477.9 1.9 bitcast_bitcast_fusion.2
  479.8 1.3 gather_fusion.1
  481.1 2.6 fusion.29
  483.8 0.6 fusion.6
  484.5 101.1 %psum.21 = f32[64]{0:T(128)S(1)} all-reduce(f32[64]{0:T(128)S(1)} %multiply_reduce_fusion.3), channel_id=1, replica_groups=mesh['region'=16,'row'=32] {'region','row'}, use_global_device_ids=true, to_apply=%region_4.5 | all-reduce | flops 64 | bytes 512 | tf_op jit(solution)/shard_map/psum | solution.py:76
  586.1 0.6 copy-done.6
  586.8 256.4 %all-reduce.9.cloned.1.call-done = f32[32768]{0:T(1024)} async-done(((f32[32768]{0:T(1024)}), f32[32768]{0:T(1024)}) %all-reduce.9.cloned.1.call-update) | async-done | bytes 131088
  843.3 1.0 reshape.423
  844.4 0.7 multiply_add_fusion.4
  845.4 1.7 collective-permute-start.2
  847.0 1.3 collective-permute-done.2
  848.4 2.4 collective-permute-done.3
  850.7 66.6 %all-gather.13.cloned.1.call-done = f32[64,8192]{1,0:T(8,128)} async-done(((f32[64,256]{1,0:T(8,128)}), f32[64,8192]{1,0:T(8,128)}) %all-gather.13.cloned.1.call-update) | async-done | bytes 2097168 | tf_op jit(solution)/shard_map/all_gather | solution.py:31
  917.3 1.9 bitcast_bitcast_fusion.1
  919.2 1.3 gather_fusion.2
  920.6 2.6 fusion.30
  923.2 0.6 fusion.4
  924.0 101.1 %psum.22 = f32[64]{0:T(128)S(1)} all-reduce(f32[64]{0:T(128)S(1)} %multiply_reduce_fusion.1), channel_id=1, replica_groups=mesh['region'=16,'row'=32] {'region','row'}, use_global_device_ids=true, to_apply=%region_8.9 | all-reduce | flops 64 | bytes 512 | tf_op jit(solution)/shard_map/psum | solution.py:76
  1025.6 0.6 copy-done.4
  1026.3 256.5 %all-reduce.11.cloned.1.call-done = f32[32768]{0:T(1024)} async-done(((f32[32768]{0:T(1024)}), f32[32768]{0:T(1024)}) %all-reduce.11.cloned.1.call-update) | async-done | bytes 131088
  1282.8 1.0 reshape.424
  1283.9 0.5 copy-done.15
  1284.4 0.7 multiply_add_fusion.2
  1285.4 1.7 collective-permute-start.4
  1287.0 1.3 collective-permute-done.4
  1288.4 2.4 collective-permute-done.5
  1290.7 66.7 %all-gather.15.cloned.1.call-done = f32[64,8192]{1,0:T(8,128)} async-done(((f32[64,256]{1,0:T(8,128)}), f32[64,8192]{1,0:T(8,128)}) %all-gather.15.cloned.1.call-update) | async-done | bytes 2097168 | tf_op jit(solution)/shard_map/all_gather | solution.py:31
  1357.5 1.9 bitcast_bitcast_fusion
  1359.4 1.6 gather_fusion.3
  1361.0 2.6 fusion.31
  1363.6 0.6 fusion.2
  1364.4 101.1 %psum.23 = f32[64]{0:T(128)S(1)} all-reduce(f32[64]{0:T(128)S(1)} %fusion.8), channel_id=1, replica_groups=mesh['region'=16,'row'=32] {'region','row'}, use_global_device_ids=true, to_apply=%region_12.13 | all-reduce | flops 64 | bytes 512 | tf_op jit(solution)/shard_map/psum | solution.py:76
  1465.6 0.8 fusion.10
  (87 shorter events, 3.4 us)
Async XLA Ops:
  7.2 474.0 %copy-start = (f32[12,128,128]{2,1,0:T(8,128)S(1)}, f32[12,128,128]{2,1,0:T(8,128)}, u32[]{:S(2)}) copy-start(f32[12,128,128]{2,1,0:T(8,128)} %param.11) | copy-start | bytes 2359300
  7.2 123.1 %all-gather.9.cloned.1.call-start = ((), (), s32[]{:S(2)}) async-start(), calls=%async_computation | async-start | bytes 2162688 | tf_op jit(solution)/shard_map/all_gather | solution.py:68
  43.3 359.9 %all-reduce.7.cloned.1.call-start = ((), (), s32[]{:S(2)}) async-start(), calls=%async_computation.4 | async-start | bytes 262144
  44.7 800.5 %copy-start.7 = (pred[256]{0:T(512)(128)(4,1)}, pred[256]{0:T(512)(128)(4,1)S(1)}, u32[]{:S(2)}) copy-start(pred[256]{0:T(512)(128)(4,1)S(1)} %compare_and_fusion.1) | copy-start | bytes 772
  44.7 94.8 %copy-start.17 = (s32[12]{0:T(128)S(1)}, s32[12]{0:T(128)}, u32[]{:S(2)}) copy-start(s32[12]{0:T(128)} %param.13) | copy-start | bytes 148
  44.7 94.8 %copy-start.14 = (s32[1,256]{1,0:T(1,128)S(1)}, s32[1,256]{1,0:T(1,128)}, u32[]{:S(2)}) copy-start(s32[1,256]{1,0:T(1,128)} %param.10) | copy-start | bytes 3076
  138.0 0.7 copy-start.5
  138.7 339.2 %all-gather.11.cloned.1.call-start = ((), (), s32[]{:S(2)}) async-start(), calls=%async_computation.1 | async-start | bytes 2162688 | tf_op jit(solution)/shard_map/all_gather | solution.py:31
  139.5 703.8 %all-reduce.9.cloned.1.call-start = ((), (), s32[]{:S(2)}) async-start(), calls=%async_computation.5 | async-start | bytes 262144
  139.6 264.8 %collective-permute-start = (f32[1,64,256]{2,1,0:T(8,128)S(1)}, f32[1,64,256]{2,1,0:T(8,128)S(1)}, u32[]{:S(2)}, u32[]{:S(2)}) collective-permute-start(f32[1,64,256]{2,1,0:T(8,128)S(1)} %bitcast_select_fusion.1), channel_id=1, source_target_pairs={{0,32},{32,64},{64,96},{96,128},{128,160},{160,192},{192,224},{224... | collective-permute-start | bytes 196616 | tf_op jit(solution)/shard_map/ppermute | solution.py:15
  144.4 260.0 %collective-permute-start.1 = (f32[1,64,256]{2,1,0:T(8,128)S(1)}, f32[1,64,256]{2,1,0:T(8,128)S(1)}, u32[]{:S(2)}, u32[]{:S(2)}) collective-permute-start(f32[1,64,256]{2,1,0:T(8,128)S(1)} %bitcast_select_fusion.1), channel_id=1, source_target_pairs={{32,0},{64,32},{96,64},{128,96},{160,128},{192,160},{224,192},{256... | collective-permute-start | bytes 196616 | tf_op jit(solution)/shard_map/ppermute | solution.py:18
  144.4 774.8 %copy-start.9 = (s32[1024]{0:T(1024)}, s32[1024]{0:T(1024)S(1)}, u32[]{:S(2)}) copy-start(s32[1024]{0:T(1024)S(1)} %pad_clamp_fusion) | copy-start | bytes 12292
  479.8 4.0 copy-start.12
  479.8 364.6 %copy-start.1 = (f32[64,256]{1,0:T(8,128)S(1)}, f32[64,256]{1,0:T(8,128)}, u32[]{:S(2)}) copy-start(f32[64,256]{1,0:T(8,128)} %get-tuple-element.15) | copy-start | bytes 196612
  586.1 0.6 copy-start.6
  586.8 330.6 %all-gather.13.cloned.1.call-start = ((), (), s32[]{:S(2)}) async-start(), calls=%async_computation.2 | async-start | bytes 2162688 | tf_op jit(solution)/shard_map/all_gather | solution.py:31
  845.1 437.7 %all-reduce.11.cloned.1.call-start = ((), (), s32[]{:S(2)}) async-start(), calls=%async_computation.6 | async-start | bytes 262144
  845.4 3.0 collective-permute-start.2
  847.0 3.7 collective-permute-start.3
  919.2 365.2 %copy-start.2 = (f32[64,256]{1,0:T(8,128)S(1)}, f32[64,256]{1,0:T(8,128)}, u32[]{:S(2)}) copy-start(f32[64,256]{1,0:T(8,128)} %multiply_add_fusion.4) | copy-start | bytes 196612
  920.5 364.7 %copy-start.8 = (pred[256]{0:T(512)(128)(4,1)S(1)}, pred[256]{0:T(512)(128)(4,1)}, u32[]{:S(2)}) copy-start(pred[256]{0:T(512)(128)(4,1)} %copy-done.7) | copy-start | bytes 772
  1025.6 0.6 copy-start.4
  1026.2 331.2 %all-gather.15.cloned.1.call-start = ((), (), s32[]{:S(2)}) async-start(), calls=%async_computation.3 | async-start | bytes 2162688 | tf_op jit(solution)/shard_map/all_gather | solution.py:31
  1283.9 0.5 copy-start.15
  1284.4 73.1 %copy-start.10 = (f32[64]{0:T(128)}, f32[64]{0:T(128)S(1)}, u32[]{:S(2)}) copy-start(f32[64]{0:T(128)S(1)} %div.26) | copy-start | bytes 772
  1285.4 3.0 collective-permute-start.4
  1287.0 3.7 collective-permute-start.5
  1359.4 4.3 copy-start.13
  1359.4 4.9 copy-start.11
  1359.4 106.2 %copy-start.16 = (f32[64]{0:T(128)S(1)}, f32[64]{0:T(128)}, u32[]{:S(2)}) copy-start(f32[64]{0:T(128)} %copy-done.15) | copy-start | bytes 772
  1359.4 106.2 %copy-start.3 = (f32[64,256]{1,0:T(8,128)S(1)}, f32[64,256]{1,0:T(8,128)}, u32[]{:S(2)}) copy-start(f32[64,256]{1,0:T(8,128)} %get-tuple-element.12) | copy-start | bytes 196612
Sparse Core Ops, SparseCore 0:
  43.4 86.7 all-gather.8
  138.8 264.3 all-reduce.6
  407.3 70.5 all-gather.10
  586.9 256.3 all-reduce.8
  846.7 70.5 all-gather.12
  1026.4 256.3 all-reduce.10
  1286.9 70.5 all-gather.14
